TPU v7x, 512 devices: a whole 4x8x8 slice. The times are simulated.
512 devices in a mesh: grp: 16 (over z, core), blk: 32 (over x, y).
Axes of the slice: x: 4, y: 8, z: 8, core: 2. Of those that a mesh axis runs over, the one named last changes fastest.
Arguments:
- leaf_blocks: float32 [16, 256, 256], P('grp'), may hold values from 0 to 5, as said below
- leaf_rhs: float32 [16, 256, 8192], P('grp', None, 'blk'), may hold values from -0.24 to 0.24
- bases: bfloat16 [16, 512, 512], P('grp'), may hold values from -1 to 2, as said below
- couplings: bfloat16 [16, 256, 256], P('grp'), may hold values from -1 to 1, as said below
Outputs:
- root_solution: float32 [256, 8192], P('grp', 'blk')
Inputs may be any that keep to these rules, and one draw needn't show every extreme that they name: `leaf_blocks`: each block is symmetric, and every merged matrix and Schur complement of the levels is positive definite. `bases`: each transform is nonsingular; slot 0 is not an owner. `couplings`: slot 0 is not an owner.
All inputs are finite; a program needn't handle non-finite values.
Results may differ from a plain program's by a relative error of at most 0.0003.
Values may be sent and summed in bfloat16 or wider, within the bound.
A program may use at most 64 MiB of HBM per device.

v0:
```python
import functools
import jax
import jax.numpy as jnp
from jax import lax
from jax.experimental import pallas as pl
from jax.experimental.pallas import tpu as pltpu
from jax.sharding import PartitionSpec as P

F32 = jnp.float32
BF16 = jnp.bfloat16
HIGH = lax.Precision.HIGHEST
LANES = 128
WIDE = 16


def reciprocal(x):
    return pl.reciprocal(x, approx=True)


def dot(a, b):
    return jnp.dot(a, b, preferred_element_type=F32)


def dot_full(a, b):
    return jnp.dot(a, b, preferred_element_type=F32, precision=HIGH)


def dot_full_t(a, b):
    return lax.dot_general(a, b, (((0,), (0,)), ((), ())), preferred_element_type=F32, precision=HIGH)


def pieces(x, count):
    out = []
    for _ in range(count - 1):
        part = x.astype(BF16)
        out.append(part)
        x = x - part.astype(F32)
    out.append(x.astype(BF16))
    return out


def eliminate(tile, size):
    tiles = WIDE // 8
    rows = tile.reshape(size // 8, 8, LANES)
    sub = lax.broadcasted_iota(jnp.int32, (8, LANES), 0)
    outs = []

    def spread(x, c):
        return jnp.broadcast_to(x[c : c + 1, :], (8, LANES))

    for start in range(0, size, WIDE):
        m = (size - start) // 8
        cols = [jnp.broadcast_to(rows[:, :, start + c : start + c + 1], (m, 8, LANES)) for c in range(WIDE)]
        pivots = [jnp.ones((8, LANES), F32) for _ in range(tiles)]
        for c in range(WIDE):
            q, cc = c // 8, c % 8
            pivot = spread(cols[c][q], cc)
            inverse = reciprocal(pivot)
            pivots[q] = jnp.where(sub == cc, pivot, pivots[q])
            head = jnp.where(sub > cc, cols[c][q], 0.0)[None]
            below = jnp.concatenate([head, cols[c][q + 1 :]], 0) if q + 1 < m else head
            for d in range(c + 1, WIDE):
                new = cols[d][q:] - below * (spread(cols[d][q], cc) * inverse)[None]
                cols[d] = jnp.concatenate([cols[d][:q], new], 0) if q else new
            new = rows[q:] - below * (spread(rows[q], cc) * inverse)[None]
            rows = jnp.concatenate([rows[:q], new], 0) if q else new
        for q in range(tiles):
            outs.append(rows[q] * lax.rsqrt(pivots[q]))
        rows = rows[tiles:]
    return jnp.concatenate(outs, 0)


def inverse_factor(a_ref, out_ref):
    h = LANES // 2
    eye = jnp.where(
        lax.broadcasted_iota(jnp.int32, (h, h), 0) == lax.broadcasted_iota(jnp.int32, (h, h), 1), 1.0, 0.0
    ).astype(F32)
    first = eliminate(jnp.concatenate([a_ref[:h, :h], eye], 1), h)[:, h:]
    reach = dot_full(first, a_ref[:h, h:])
    rest = a_ref[h:, h:] - dot_full_t(reach, reach)
    second = eliminate(jnp.concatenate([rest, eye], 1), h)[:, h:]
    corner = -dot_full(second, dot_full_t(reach, first))
    out_ref[:h, :] = jnp.concatenate([first, jnp.zeros((h, h), F32)], 1)
    out_ref[h:, :] = jnp.concatenate([corner, second], 1)


def kernel(
    groups, rank, leaf_s, leaf_y, base, link, out,
    s_in, y_in, w, w_t, b, mix, cross, upper, akk, linv, reach, vee, s_out, y_out, xs, rows_in,
    local_sem, s_send, s_recv, y_send, y_recv, leaf_send, x_send, x_recv,
):
    me = lax.axis_index("grp")
    half = rank // 2
    root = groups // 2
    share = rank // groups
    odd = lax.rem(me, 2) == 1
    step = jnp.int32(1)
    bits = groups.bit_length() - 1
    for bit in range(bits):
        step = jnp.where(lax.rem(me, 2 << bit) == 1 << bit, 1 << bit, step)
    second = lax.rem(me // (2 * step), 2)
    target = me + step - 2 * step * second

    def remote(src, dst, send, recv, group):
        return pltpu.make_async_remote_copy(
            src_ref=src, dst_ref=dst, send_sem=send, recv_sem=recv,
            device_id={"grp": group}, device_id_type=pl.DeviceIdType.MESH,
        )

    cuts = ((pl.ds(0, half), pl.ds(0, rank)), (pl.ds(half, half), pl.ds(half, half)))

    def s_copies(src, sems, slot, group):
        return [
            remote(src.at[cut], s_in.at[(slot, *cut)], sems.at[k], s_recv.at[slot, k], group)
            for k, cut in enumerate(cuts)
        ]

    leaf_s_copies = s_copies(leaf_s.at[0], leaf_send, 0, me + 1)
    leaf_y_copy = remote(leaf_y.at[0], y_in.at[0], leaf_send.at[2], y_recv.at[0], me + 1)
    up_s_copies = s_copies(s_out, s_send, second, target)
    up_y_copy = remote(y_out, y_in.at[second], y_send, y_recv.at[second], target)
    own_s = pltpu.make_async_copy(leaf_s.at[0], s_in.at[1], local_sem.at[0])
    own_y = pltpu.make_async_copy(leaf_y.at[0], y_in.at[1], local_sem.at[1])
    own_w = pltpu.make_async_copy(base.at[0], w, local_sem.at[2])
    own_b = pltpu.make_async_copy(link.at[0], b, local_sem.at[3])

    barrier = pltpu.get_barrier_semaphore()

    def greet(group):
        pl.semaphore_signal(barrier, inc=1, device_id={"grp": group}, device_id_type=pl.DeviceIdType.MESH)

    @pl.when(odd)
    def _():
        greet(me - 1)
        own_s.start()

    for bit in range(1, bits):
        @pl.when(lax.rem(me, 2 << bit) == 1 << bit)
        def _():
            lean = 0 if bit == 1 else 1
            greet(me - (1 << bit) // 2 + lean)
            greet(me + (1 << bit) // 2 + lean)

    @pl.when(jnp.logical_not(odd))
    def _():
        pl.semaphore_wait(barrier, 1)
        for copy in leaf_s_copies:
            copy.start()
        leaf_y_copy.start()

    own_w.start()
    own_b.start()

    @pl.when(odd)
    def _():
        own_y.start()

    own_w.wait()
    own_b.wait()

    def factor():
        def turn(part, carry):
            inverse_factor(akk, linv.at[part])

            @pl.when(part == 0)
            def _():
                reach[...] = dot_full(linv[0], upper[:half, half:])
                rest = upper[half:rank, half:] - dot_full_t(reach[:, :half], reach[...])
                akk[...] = rest[:, :half]
                vee[:half, :] = reach[:, half:]
                vee[half:, :] = rest[:, half:]

            return carry

        lax.fori_loop(0, 2, turn, 0)

    @pl.when(me > 0)
    def _():
        w_t[...] = w[...].T
        cross[:rank, :] = dot(b[...], w[rank:, :])
        cross[rank:, :] = lax.dot_general(b[...], w[:rank, :], (((0,), (0,)), ((), ())), preferred_element_type=F32)
        for copy in s_copies(s_out, s_send, 0, target):
            copy.wait_recv()

        @pl.when(odd)
        def _():
            own_s.wait()

        @pl.when(jnp.logical_not(odd))
        def _():
            for copy in s_copies(s_out, s_send, 1, target):
                copy.wait_recv()

        for slot in (0, 1):
            at = slot * rank
            s_in[slot, half:, :half] = s_in[slot, :half, half:].T
            hi, mid, low = pieces(s_in[slot], 3)
            own = w[at : at + rank, :]
            mix[at : at + rank, :] = dot(low, own) + dot(mid, own) + cross[at : at + rank, :] + dot(hi, own)
        hi, mid, low = pieces(mix[...], 3)
        upper[:rank, :] = dot(w_t[:rank, :], low) + dot(w_t[:rank, :], mid) + dot(w_t[:rank, :], hi)
        lower = w_t[rank:, :]
        upper[rank:, rank:] = dot(lower, low[:, rank:]) + dot(lower, mid[:, rank:]) + dot(lower, hi[:, rank:])
        akk[...] = upper[:half, :half]
        factor()
        vee[half:, :] = dot_full(linv[1], vee[half:, :])

        @pl.when(odd)
        def _():
            extra = lax.rem(me, 4) == 3
            for bit in range(3, bits):
                for sign in (-1, 1):
                    for owner in range(1 << bit, groups, 2 << bit):
                        extra = extra | (me == owner + sign * (1 << bit) // 2 + 1)
            pl.semaphore_wait(barrier, jnp.where(extra, 2, 1))

        s_out[:half, :] = upper[rank : rank + half, rank:] - dot_full_t(vee[:, :half], vee[...])

        @pl.when(me != root)
        def _():
            up_s_copies[0].start()

        s_out[half:, half:] = upper[rank + half :, rank + half :] - dot_full_t(vee[:, half:], vee[:, half:])

        @pl.when(me != root)
        def _():
            up_s_copies[1].start()

        remote(y_out, y_in.at[0], y_send, y_recv.at[0], target).wait_recv()

        @pl.when(odd)
        def _():
            own_y.wait()

        @pl.when(jnp.logical_not(odd))
        def _():
            remote(y_out, y_in.at[1], y_send, y_recv.at[1], target).wait_recv()

        mixed = jnp.zeros((2 * rank, y_in.shape[2]), F32)
        for slot in (0, 1):
            hi, mid, low = pieces(y_in[slot], 3)
            cut = w_t[:, slot * rank : (slot + 1) * rank]
            mixed = mixed + (dot(cut, low) + dot(cut, mid) + dot(cut, hi))
        top = dot_full(linv[0], mixed[:half])
        low = dot_full(linv[1], mixed[half:rank] - dot_full_t(reach[:, :half], top))
        y_out[...] = mixed[rank:] - dot_full_t(vee[...], jnp.concatenate([top, low], 0))

        @pl.when(me != root)
        def _():
            up_y_copy.start()

    def x_copy(group):
        return remote(xs.at[pl.ds(group * share, share), :], rows_in, x_send.at[group], x_recv, group)

    @pl.when(me == root)
    def _():
        s_out[half:, :half] = s_out[:half, half:].T
        upper[:rank, :rank] = s_out[...]
        akk[...] = s_out[:half, :half]
        factor()
        top = dot_full(linv[0], y_out[:half])
        low = dot_full(linv[1], y_out[half:] - dot_full_t(reach[:, :half], top))
        low = dot_full_t(linv[1], low)
        xs[half:, :] = low
        xs[:half, :] = dot_full_t(linv[0], top - dot_full(reach[:, :half], low))
        for group in range(groups):
            if group != root:
                x_copy(group).start()
        out[...] = xs[root * share : (root + 1) * share, :]
        for group in range(groups):
            if group != root:
                x_copy(group).wait_send()

    @pl.when(me != root)
    def _():
        @pl.when(me > 0)
        def _():
            for copy in up_s_copies:
                copy.wait_send()
            up_y_copy.wait_send()

    @pl.when(jnp.logical_not(odd))
    def _():
        for copy in leaf_s_copies:
            copy.wait_send()
        leaf_y_copy.wait_send()

    @pl.when(me != root)
    def _():
        x_copy(0 if root else 1).wait_recv()
        out[...] = rows_in[...]


def body(leaf_blocks, leaf_rhs, bases, couplings):
    groups = lax.axis_size("grp")
    rank = leaf_blocks.shape[1]
    width = leaf_rhs.shape[2]
    outside = pl.BlockSpec(memory_space=pltpu.HBM)
    return pl.pallas_call(
        functools.partial(kernel, groups, rank),
        out_shape=jax.ShapeDtypeStruct((rank // groups, width), F32),
        in_specs=[outside] * 4,
        out_specs=pl.BlockSpec(memory_space=pltpu.VMEM),
        scratch_shapes=[
            pltpu.VMEM((2, rank, rank), F32),
            pltpu.VMEM((2, rank, width), F32),
            pltpu.VMEM((2 * rank, 2 * rank), BF16),
            pltpu.VMEM((2 * rank, 2 * rank), BF16),
            pltpu.VMEM((rank, rank), BF16),
            pltpu.VMEM((2 * rank, 2 * rank), F32),
            pltpu.VMEM((2 * rank, 2 * rank), F32),
            pltpu.VMEM((2 * rank, 2 * rank), F32),
            pltpu.VMEM((rank // 2, rank // 2), F32),
            pltpu.VMEM((2, rank // 2, rank // 2), F32),
            pltpu.VMEM((rank // 2, 3 * rank // 2), F32),
            pltpu.VMEM((rank, rank), F32),
            pltpu.VMEM((rank, rank), F32),
            pltpu.VMEM((rank, width), F32),
            pltpu.VMEM((rank, width), F32),
            pltpu.VMEM((rank // groups, width), F32),
            pltpu.SemaphoreType.DMA((4,)),
            pltpu.SemaphoreType.DMA((2,)),
            pltpu.SemaphoreType.DMA((2, 2)),
            pltpu.SemaphoreType.DMA,
            pltpu.SemaphoreType.DMA((2,)),
            pltpu.SemaphoreType.DMA((3,)),
            pltpu.SemaphoreType.DMA((groups,)),
            pltpu.SemaphoreType.DMA,
        ],
        compiler_params=pltpu.CompilerParams(
            collective_id=0, has_side_effects=True, vmem_limit_bytes=63 << 20
        ),
    )(leaf_blocks, leaf_rhs, bases, couplings)


def solution(mesh):
    placed = (
        P("grp", None, None),
        P("grp", None, "blk"),
        P("grp", None, None),
        P("grp", None, None),
    )
    return jax.shard_map(
        body, mesh=mesh, in_specs=placed, out_specs=P("grp", "blk"), check_vma=False
    )
```

profile of v0, /device:TPU:1, one launch (start us, length us, event | category | flops | bytes accessed | tf_op | source)
XLA Modules:
  0.0 84.2 jit_solution(15111246281609305235)
XLA Ops:
  0.0 82.9 %shard_map.46 = f32[16,256]{1,0:T(8,128)} custom-call(f32[1,256,256]{2,1,0:T(8,128)} %leaf_s.1, f32[1,256,256]{2,1,0:T(8,128)} %leaf_y.1, bf16[1,512,512]{2,1,0:T(8,128)(2,1)} %base.1, bf16[1,256,256]{2,1,0:T(8,128)(2,1)} %link.1), custom_call_target="tpu_custom_call" | custom-call | tf_op jit(solution)/shard_map/pallas_call | solution.py:299
  82.9 1.3 %copy.6 = f32[16,256]{1,0:T(8,128)} copy(f32[16,256]{1,0:T(8,128)} %shard_map.46) | data formatting | bytes 32768
where the time goes:
time: 84.4 us; the launch traced here: 84.2 us
  Pallas kernels  82.9 us (98%)
  local copies, waits for them, and re-layouts  1.32 us (2%)
    pallas_call x1, Pallas kernels, body(): pl.pallas_call(functools.partial(kernel, groups, rank), out_shape=jax.Sha...  82.9 us

commit v1 on v0

--- a/solution.py
+++ b/solution.py
@@ -10,7 +10,6 @@
 BF16 = jnp.bfloat16
 HIGH = lax.Precision.HIGHEST
 LANES = 128
-WIDE = 16
 
 
 def reciprocal(x):
@@ -27,6 +26,14 @@
 
 def dot_full_t(a, b):
     return lax.dot_general(a, b, (((0,), (0,)), ((), ())), preferred_element_type=F32, precision=HIGH)
+
+
+def dot_near(a, b, contract=1):
+    a_hi, a_low = pieces(a, 2)
+    b_hi, b_low = pieces(b, 2)
+    dims = (((contract,), (0,)), ((), ()))
+    product = functools.partial(lax.dot_general, dimension_numbers=dims, preferred_element_type=F32)
+    return product(a_low, b_hi) + product(a_hi, b_low) + product(a_hi, b_hi)
 
 
 def pieces(x, count):
@@ -39,54 +46,48 @@
     return out
 
 
-def eliminate(tile, size):
-    tiles = WIDE // 8
-    rows = tile.reshape(size // 8, 8, LANES)
+def eliminate(rows, size, at):
+    rows = rows.reshape(size // 8, 8, LANES)
     sub = lax.broadcasted_iota(jnp.int32, (8, LANES), 0)
     outs = []
 
     def spread(x, c):
         return jnp.broadcast_to(x[c : c + 1, :], (8, LANES))
 
-    for start in range(0, size, WIDE):
+    for start in range(0, size, 8):
         m = (size - start) // 8
-        cols = [jnp.broadcast_to(rows[:, :, start + c : start + c + 1], (m, 8, LANES)) for c in range(WIDE)]
-        pivots = [jnp.ones((8, LANES), F32) for _ in range(tiles)]
-        for c in range(WIDE):
-            q, cc = c // 8, c % 8
-            pivot = spread(cols[c][q], cc)
-            inverse = reciprocal(pivot)
-            pivots[q] = jnp.where(sub == cc, pivot, pivots[q])
-            head = jnp.where(sub > cc, cols[c][q], 0.0)[None]
-            below = jnp.concatenate([head, cols[c][q + 1 :]], 0) if q + 1 < m else head
-            for d in range(c + 1, WIDE):
-                new = cols[d][q:] - below * (spread(cols[d][q], cc) * inverse)[None]
-                cols[d] = jnp.concatenate([cols[d][:q], new], 0) if q else new
-            new = rows[q:] - below * (spread(rows[q], cc) * inverse)[None]
-            rows = jnp.concatenate([rows[:q], new], 0) if q else new
-        for q in range(tiles):
-            outs.append(rows[q] * lax.rsqrt(pivots[q]))
-        rows = rows[tiles:]
+        cols = [jnp.broadcast_to(rows[:, :, at + start + c : at + start + c + 1], (m, 8, LANES)) for c in range(8)]
+        pivots = jnp.ones((8, LANES), F32)
+        for c in range(0, 8, 2):
+            a, b, d = spread(cols[c][0], c), spread(cols[c + 1][0], c), spread(cols[c + 1][0], c + 1)
+            det = a * d - b * b
+            over_det, over_a = reciprocal(det), reciprocal(a)
+            pivots = jnp.where(sub == c, a, jnp.where(sub == c + 1, det * over_a, pivots))
+
+            def below(x):
+                head = jnp.where(sub > c + 1, x[0], 0.0)[None]
+                return jnp.concatenate([head, x[1:]], 0) if m > 1 else head
+
+            left, right = below(cols[c]), below(cols[c + 1])
+
+            def reduced(x, u, v):
+                f, g = (d * u - b * v) * over_det, (a * v - b * u) * over_det
+                return x - (left * f[None] + right * g[None])
+
+            for e in range(c + 2, 8):
+                cols[e] = reduced(cols[e], spread(cols[e][0], c), spread(cols[e][0], c + 1))
+            u = spread(rows[0], c)
+            rows = reduced(rows, u, spread(rows[0], c + 1))
+            head = jnp.where(sub == c + 1, rows[0] - (b * over_a) * u, rows[0])[None]
+            rows = jnp.concatenate([head, rows[1:]], 0) if m > 1 else head
+        outs.append(rows[0] * lax.rsqrt(pivots))
+        rows = rows[1:]
     return jnp.concatenate(outs, 0)
-
-
-def inverse_factor(a_ref, out_ref):
-    h = LANES // 2
-    eye = jnp.where(
-        lax.broadcasted_iota(jnp.int32, (h, h), 0) == lax.broadcasted_iota(jnp.int32, (h, h), 1), 1.0, 0.0
-    ).astype(F32)
-    first = eliminate(jnp.concatenate([a_ref[:h, :h], eye], 1), h)[:, h:]
-    reach = dot_full(first, a_ref[:h, h:])
-    rest = a_ref[h:, h:] - dot_full_t(reach, reach)
-    second = eliminate(jnp.concatenate([rest, eye], 1), h)[:, h:]
-    corner = -dot_full(second, dot_full_t(reach, first))
-    out_ref[:h, :] = jnp.concatenate([first, jnp.zeros((h, h), F32)], 1)
-    out_ref[h:, :] = jnp.concatenate([corner, second], 1)
 
 
 def kernel(
     groups, rank, leaf_s, leaf_y, base, link, out,
-    s_in, y_in, w, w_t, b, mix, cross, upper, akk, linv, reach, vee, s_out, y_out, xs, rows_in,
+    s_in, y_in, w, w_t, b, mix, cross, upper, panel, blocks, lead, trail, joint, linv, reach, vee, s_out, y_out, xs, rows_in,
     local_sem, s_send, s_recv, y_send, y_recv, leaf_send, x_send, x_recv,
 ):
     me = lax.axis_index("grp")
@@ -158,21 +159,43 @@
     own_w.wait()
     own_b.wait()
 
+    small = half // 2
+    same = lax.broadcasted_iota(jnp.int32, (small, half), 0) == lax.rem(lax.broadcasted_iota(jnp.int32, (small, half), 1), small)
+    lane = lax.broadcasted_iota(jnp.int32, (small, half), 1)
+    eye = jnp.where(same, 1.0, 0.0).astype(F32)
+
     def factor():
+        panel[:, :half] = upper[:half, :half]
+        panel[:, half:] = upper[:half, half:]
+
         def turn(part, carry):
-            inverse_factor(akk, linv.at[part])
+            first = eliminate(jnp.where(lane < small, panel[:small, :half], eye), small, 0)[:, small:]
+            lead[part] = first
+            top = dot_full(first, panel[:small, :])
+            joint[part] = top[:, :half]
+            rest = panel[small:, :] - dot_full_t(top[:, small:half], top)
+            second = eliminate(jnp.where(lane < small, eye, rest[:, :half]), small, small)[:, :small]
+            trail[part] = second
+            low = dot_full(second, rest[:, half:])
+            blocks[:small, :] = top[:, half:]
+            blocks[small:, :] = low
+            vee[pl.ds(pl.multiple_of(part * half, half), half), :] = blocks[:, half:]
 
             @pl.when(part == 0)
             def _():
-                reach[...] = dot_full(linv[0], upper[:half, half:])
-                rest = upper[half:rank, half:] - dot_full_t(reach[:, :half], reach[...])
-                akk[...] = rest[:, :half]
-                vee[:half, :] = reach[:, half:]
-                vee[half:, :] = rest[:, half:]
+                reach[...] = blocks[:, :half]
+                panel[:, :half] = upper[half:rank, half:rank] - dot_full_t(reach[...], reach[...])
+                panel[:, rank:] = upper[half:rank, rank:] - dot_full_t(reach[...], vee[:half, :])
 
             return carry
 
         lax.fori_loop(0, 2, turn, 0)
+
+    def inverses(parts):
+        for part in parts:
+            corner = dot_near(trail[part], dot_near(joint[part], lead[part], 0)[small:])
+            linv[part, :small, :] = jnp.concatenate([lead[part], jnp.zeros((small, small), F32)], 1)
+            linv[part, small:, :] = jnp.concatenate([-corner, trail[part]], 1)
 
     @pl.when(me > 0)
     def _():
@@ -201,9 +224,7 @@
         upper[:rank, :] = dot(w_t[:rank, :], low) + dot(w_t[:rank, :], mid) + dot(w_t[:rank, :], hi)
         lower = w_t[rank:, :]
         upper[rank:, rank:] = dot(lower, low[:, rank:]) + dot(lower, mid[:, rank:]) + dot(lower, hi[:, rank:])
-        akk[...] = upper[:half, :half]
         factor()
-        vee[half:, :] = dot_full(linv[1], vee[half:, :])
 
         @pl.when(odd)
         def _():
@@ -236,14 +257,15 @@
         def _():
             remote(y_out, y_in.at[1], y_send, y_recv.at[1], target).wait_recv()
 
+        inverses((0, 1))
         mixed = jnp.zeros((2 * rank, y_in.shape[2]), F32)
         for slot in (0, 1):
-            hi, mid, low = pieces(y_in[slot], 3)
+            hi, low = pieces(y_in[slot], 2)
             cut = w_t[:, slot * rank : (slot + 1) * rank]
-            mixed = mixed + (dot(cut, low) + dot(cut, mid) + dot(cut, hi))
-        top = dot_full(linv[0], mixed[:half])
-        low = dot_full(linv[1], mixed[half:rank] - dot_full_t(reach[:, :half], top))
-        y_out[...] = mixed[rank:] - dot_full_t(vee[...], jnp.concatenate([top, low], 0))
+            mixed = mixed + (dot(cut, low) + dot(cut, hi))
+        top = dot_near(linv[0], mixed[:half])
+        low = dot_near(linv[1], mixed[half:rank] - dot_near(reach[...], top, 0))
+        y_out[...] = mixed[rank:] - dot_near(vee[...], jnp.concatenate([top, low], 0), 0)
 
         @pl.when(me != root)
         def _():
@@ -256,13 +278,12 @@
     def _():
         s_out[half:, :half] = s_out[:half, half:].T
         upper[:rank, :rank] = s_out[...]
-        akk[...] = s_out[:half, :half]
+        upper[:rank, rank:] = y_out[...]
         factor()
-        top = dot_full(linv[0], y_out[:half])
-        low = dot_full(linv[1], y_out[half:] - dot_full_t(reach[:, :half], top))
-        low = dot_full_t(linv[1], low)
+        inverses((1, 0))
+        low = dot_near(linv[1], vee[half:, :], 0)
         xs[half:, :] = low
-        xs[:half, :] = dot_full_t(linv[0], top - dot_full(reach[:, :half], low))
+        xs[:half, :] = dot_near(linv[0], vee[:half, :] - dot_near(reach[...], low), 0)
         for group in range(groups):
             if group != root:
                 x_copy(group).start()
@@ -310,9 +331,13 @@
             pltpu.VMEM((2 * rank, 2 * rank), F32),
             pltpu.VMEM((2 * rank, 2 * rank), F32),
             pltpu.VMEM((2 * rank, 2 * rank), F32),
+            pltpu.VMEM((rank // 2, 2 * rank), F32),
+            pltpu.VMEM((rank // 2, 3 * rank // 2), F32),
+            pltpu.VMEM((2, rank // 4, rank // 4), F32),
+            pltpu.VMEM((2, rank // 4, rank // 4), F32),
+            pltpu.VMEM((2, rank // 4, rank // 2), F32),
+            pltpu.VMEM((2, rank // 2, rank // 2), F32),
             pltpu.VMEM((rank // 2, rank // 2), F32),
-            pltpu.VMEM((2, rank // 2, rank // 2), F32),
-            pltpu.VMEM((rank // 2, 3 * rank // 2), F32),
             pltpu.VMEM((rank, rank), F32),
             pltpu.VMEM((rank, rank), F32),
             pltpu.VMEM((rank, width), F32),

time: 84.4 us -> 75.5 us (0.89)
  Pallas kernels: 82.9 us -> 74 us
    pallas_call x1, Pallas kernels: 82.9 us -> 74 us  [body(): pl.pallas_call(functools.partial(kernel, groups, rank), out_shape=jax.Sha...]
where the time goes in v1:
time: 75.5 us; the launch traced here: 75.4 us
  Pallas kernels  74 us (98%)
  local copies, waits for them, and re-layouts  1.32 us (2%)
    pallas_call x1, Pallas kernels, body(): pl.pallas_call(functools.partial(kernel, groups, rank), out_shape=jax.Sha...  74 us

profile of v1, /device:TPU:1, one launch (start us, length us, event | category | flops | bytes accessed | tf_op | source)
XLA Modules:
  0.0 75.4 jit_solution(5816409256735140521)
XLA Ops:
  0.0 74.0 %shard_map.46 = f32[16,256]{1,0:T(8,128)} custom-call(f32[1,256,256]{2,1,0:T(8,128)} %leaf_s.1, f32[1,256,256]{2,1,0:T(8,128)} %leaf_y.1, bf16[1,512,512]{2,1,0:T(8,128)(2,1)} %base.1, bf16[1,256,256]{2,1,0:T(8,128)(2,1)} %link.1), custom_call_target="tpu_custom_call" | custom-call | tf_op jit(solution)/shard_map/pallas_call | solution.py:320
  74.0 1.3 %copy.6 = f32[16,256]{1,0:T(8,128)} copy(f32[16,256]{1,0:T(8,128)} %shard_map.46) | data formatting | bytes 32768

commit v2 on v1

--- a/solution.py
+++ b/solution.py
@@ -54,9 +54,16 @@
     def spread(x, c):
         return jnp.broadcast_to(x[c : c + 1, :], (8, LANES))
 
+    def lanes(x, first):
+        return [jnp.broadcast_to(x[:, :, first + c : first + c + 1], x.shape) for c in range(8)]
+
+    head = lanes(rows[:1], at)
     for start in range(0, size, 8):
         m = (size - start) // 8
-        cols = [jnp.broadcast_to(rows[:, :, at + start + c : at + start + c + 1], (m, 8, LANES)) for c in range(8)]
+        cols = head
+        if m > 1:
+            cols = [jnp.concatenate([h, t], 0) for h, t in zip(head, lanes(rows[1:], at + start))]
+            head = lanes(rows[1:2], at + start + 8)
         pivots = jnp.ones((8, LANES), F32)
         for c in range(0, 8, 2):
             a, b, d = spread(cols[c][0], c), spread(cols[c + 1][0], c), spread(cols[c + 1][0], c + 1)
@@ -65,21 +72,26 @@
             pivots = jnp.where(sub == c, a, jnp.where(sub == c + 1, det * over_a, pivots))
 
             def below(x):
-                head = jnp.where(sub > c + 1, x[0], 0.0)[None]
-                return jnp.concatenate([head, x[1:]], 0) if m > 1 else head
+                h = jnp.where(sub > c + 1, x[0], 0.0)[None]
+                return jnp.concatenate([h, x[1:]], 0) if m > 1 else h
 
             left, right = below(cols[c]), below(cols[c + 1])
 
-            def reduced(x, u, v):
-                f, g = (d * u - b * v) * over_det, (a * v - b * u) * over_det
-                return x - (left * f[None] + right * g[None])
-
+            def factors(u, v):
+                return (d * u - b * v) * over_det, (a * v - b * u) * over_det
+
+            f, g = factors(left[0], right[0])
             for e in range(c + 2, 8):
-                cols[e] = reduced(cols[e], spread(cols[e][0], c), spread(cols[e][0], c + 1))
+                cols[e] = cols[e] - (left * spread(f, e)[None] + right * spread(g, e)[None])
+            if m > 1:
+                f, g = factors(left[1], right[1])
+                for e in range(8):
+                    head[e] = head[e] - (left[1:2] * spread(f, e)[None] + right[1:2] * spread(g, e)[None])
             u = spread(rows[0], c)
-            rows = reduced(rows, u, spread(rows[0], c + 1))
-            head = jnp.where(sub == c + 1, rows[0] - (b * over_a) * u, rows[0])[None]
-            rows = jnp.concatenate([head, rows[1:]], 0) if m > 1 else head
+            f, g = factors(u, spread(rows[0], c + 1))
+            rows = rows - (left * f[None] + right * g[None])
+            h = jnp.where(sub == c + 1, rows[0] - (b * over_a) * u, rows[0])[None]
+            rows = jnp.concatenate([h, rows[1:]], 0) if m > 1 else h
         outs.append(rows[0] * lax.rsqrt(pivots))
         rows = rows[1:]
     return jnp.concatenate(outs, 0)
@@ -87,7 +99,7 @@
 
 def kernel(
     groups, rank, leaf_s, leaf_y, base, link, out,
-    s_in, y_in, w, w_t, b, mix, cross, upper, panel, blocks, lead, trail, joint, linv, reach, vee, s_out, y_out, xs, rows_in,
+    s_in, y_in, w, w_t, b, mix, cross, upper, lead, trail, joint, linv, reach, vee, s_out, y_out, xs, rows_in,
     local_sem, s_send, s_recv, y_send, y_recv, leaf_send, x_send, x_recv,
 ):
     me = lax.axis_index("grp")
@@ -165,31 +177,29 @@
     eye = jnp.where(same, 1.0, 0.0).astype(F32)
 
     def factor():
-        panel[:, :half] = upper[:half, :half]
-        panel[:, half:] = upper[:half, half:]
-
-        def turn(part, carry):
-            first = eliminate(jnp.where(lane < small, panel[:small, :half], eye), small, 0)[:, small:]
+        diag = upper[:half, :half]
+        for part in (0, 1):
+            first = eliminate(jnp.where(lane < small, diag[:small], eye), small, 0)[:, small:]
             lead[part] = first
-            top = dot_full(first, panel[:small, :])
-            joint[part] = top[:, :half]
-            rest = panel[small:, :] - dot_full_t(top[:, small:half], top)
-            second = eliminate(jnp.where(lane < small, eye, rest[:, :half]), small, small)[:, :small]
+            top = dot_full(first, diag[:small])
+            joint[part] = top
+            rest = diag[small:] - dot_full_t(top[:, small:], top)
+            second = eliminate(jnp.where(lane < small, eye, rest), small, small)[:, :small]
             trail[part] = second
-            low = dot_full(second, rest[:, half:])
-            blocks[:small, :] = top[:, half:]
-            blocks[small:, :] = low
-            vee[pl.ds(pl.multiple_of(part * half, half), half), :] = blocks[:, half:]
-
-            @pl.when(part == 0)
-            def _():
-                reach[...] = blocks[:, :half]
-                panel[:, :half] = upper[half:rank, half:rank] - dot_full_t(reach[...], reach[...])
-                panel[:, rank:] = upper[half:rank, rank:] - dot_full_t(reach[...], vee[:half, :])
-
-            return carry
-
-        lax.fori_loop(0, 2, turn, 0)
+            if part == 0:
+                side = upper[:half, half:rank]
+                across = dot_full(first, side[:small])
+                low = dot_full(second, side[small:] - dot_full_t(top[:, small:], across))
+                reach[:small, :] = across
+                reach[small:, :] = low
+                diag = upper[half:rank, half:rank] - dot_full_t(reach[...], reach[...])
+                side = upper[:half, rank:]
+            else:
+                side = upper[half:rank, rank:] - dot_full_t(reach[...], vee[:half, :])
+            across = dot_full(first, side[:small])
+            low = dot_full(second, side[small:] - dot_full_t(top[:, small:], across))
+            vee[part * half : part * half + small, :] = across
+            vee[part * half + small : (part + 1) * half, :] = low
 
     def inverses(parts):
         for part in parts:
@@ -197,66 +207,7 @@
             linv[part, :small, :] = jnp.concatenate([lead[part], jnp.zeros((small, small), F32)], 1)
             linv[part, small:, :] = jnp.concatenate([-corner, trail[part]], 1)
 
-    @pl.when(me > 0)
-    def _():
-        w_t[...] = w[...].T
-        cross[:rank, :] = dot(b[...], w[rank:, :])
-        cross[rank:, :] = lax.dot_general(b[...], w[:rank, :], (((0,), (0,)), ((), ())), preferred_element_type=F32)
-        for copy in s_copies(s_out, s_send, 0, target):
-            copy.wait_recv()
-
-        @pl.when(odd)
-        def _():
-            own_s.wait()
-
-        @pl.when(jnp.logical_not(odd))
-        def _():
-            for copy in s_copies(s_out, s_send, 1, target):
-                copy.wait_recv()
-
-        for slot in (0, 1):
-            at = slot * rank
-            s_in[slot, half:, :half] = s_in[slot, :half, half:].T
-            hi, mid, low = pieces(s_in[slot], 3)
-            own = w[at : at + rank, :]
-            mix[at : at + rank, :] = dot(low, own) + dot(mid, own) + cross[at : at + rank, :] + dot(hi, own)
-        hi, mid, low = pieces(mix[...], 3)
-        upper[:rank, :] = dot(w_t[:rank, :], low) + dot(w_t[:rank, :], mid) + dot(w_t[:rank, :], hi)
-        lower = w_t[rank:, :]
-        upper[rank:, rank:] = dot(lower, low[:, rank:]) + dot(lower, mid[:, rank:]) + dot(lower, hi[:, rank:])
-        factor()
-
-        @pl.when(odd)
-        def _():
-            extra = lax.rem(me, 4) == 3
-            for bit in range(3, bits):
-                for sign in (-1, 1):
-                    for owner in range(1 << bit, groups, 2 << bit):
-                        extra = extra | (me == owner + sign * (1 << bit) // 2 + 1)
-            pl.semaphore_wait(barrier, jnp.where(extra, 2, 1))
-
-        s_out[:half, :] = upper[rank : rank + half, rank:] - dot_full_t(vee[:, :half], vee[...])
-
-        @pl.when(me != root)
-        def _():
-            up_s_copies[0].start()
-
-        s_out[half:, half:] = upper[rank + half :, rank + half :] - dot_full_t(vee[:, half:], vee[:, half:])
-
-        @pl.when(me != root)
-        def _():
-            up_s_copies[1].start()
-
-        remote(y_out, y_in.at[0], y_send, y_recv.at[0], target).wait_recv()
-
-        @pl.when(odd)
-        def _():
-            own_y.wait()
-
-        @pl.when(jnp.logical_not(odd))
-        def _():
-            remote(y_out, y_in.at[1], y_send, y_recv.at[1], target).wait_recv()
-
+    def side_work():
         inverses((0, 1))
         mixed = jnp.zeros((2 * rank, y_in.shape[2]), F32)
         for slot in (0, 1):
@@ -267,8 +218,74 @@
         low = dot_near(linv[1], mixed[half:rank] - dot_near(reach[...], top, 0))
         y_out[...] = mixed[rank:] - dot_near(vee[...], jnp.concatenate([top, low], 0), 0)
 
+    @pl.when(me > 0)
+    def _():
+        w_t[...] = w[...].T
+        cross[:rank, :] = dot(b[...], w[rank:, :])
+        cross[rank:, :] = lax.dot_general(b[...], w[:rank, :], (((0,), (0,)), ((), ())), preferred_element_type=F32)
+        for slot in (1, 0):
+            at = slot * rank
+            arrivals = s_copies(s_out, s_send, slot, target)
+            for k in (0, 1):
+                if slot == 0:
+                    arrivals[k].wait_recv()
+                else:
+                    @pl.when(jnp.logical_not(odd))
+                    def _():
+                        arrivals[k].wait_recv()
+
+                    if k == 0:
+                        @pl.when(odd)
+                        def _():
+                            own_s.wait()
+
+                if k == 1:
+                    s_in[slot, half:, :half] = s_in[slot, :half, half:].T
+                now = slice(at + k * half, at + (k + 1) * half)
+                hi, mid, low = pieces(s_in[slot, k * half : (k + 1) * half, :], 3)
+                own = w[at : at + rank, :]
+                mix[now, :] = dot(low, own) + dot(mid, own) + cross[now, :] + dot(hi, own)
+        hi, mid, low = pieces(mix[:, :rank], 3)
+        upper[:rank, :rank] = dot(w_t[:rank, :], low) + dot(w_t[:rank, :], mid) + dot(w_t[:rank, :], hi)
+        hi, mid, low = pieces(mix[:, rank:], 3)
+        upper[:rank, rank:] = dot(w_t[:rank, :], low) + dot(w_t[:rank, :], mid) + dot(w_t[:rank, :], hi)
+        upper[rank:, rank:] = dot(w_t[rank:, :], low) + dot(w_t[rank:, :], mid) + dot(w_t[rank:, :], hi)
+        factor()
+
+        @pl.when(odd)
+        def _():
+            extra = lax.rem(me, 4) == 3
+            for bit in range(3, bits):
+                for sign in (-1, 1):
+                    for owner in range(1 << bit, groups, 2 << bit):
+                        extra = extra | (me == owner + sign * (1 << bit) // 2 + 1)
+            pl.semaphore_wait(barrier, jnp.where(extra, 2, 1))
+
+        s_out[:half, :] = upper[rank : rank + half, rank:] - dot_full_t(vee[:, :half], vee[...])
+
         @pl.when(me != root)
         def _():
+            up_s_copies[0].start()
+
+        s_out[half:, half:] = upper[rank + half :, rank + half :] - dot_full_t(vee[:, half:], vee[:, half:])
+
+        @pl.when(me != root)
+        def _():
+            up_s_copies[1].start()
+
+        remote(y_out, y_in.at[0], y_send, y_recv.at[0], target).wait_recv()
+
+        @pl.when(odd)
+        def _():
+            own_y.wait()
+
+        @pl.when(jnp.logical_not(odd))
+        def _():
+            remote(y_out, y_in.at[1], y_send, y_recv.at[1], target).wait_recv()
+
+        @pl.when(me != root)
+        def _():
+            side_work()
             up_y_copy.start()
 
     def x_copy(group):
@@ -276,6 +293,7 @@
 
     @pl.when(me == root)
     def _():
+        side_work()
         s_out[half:, :half] = s_out[:half, half:].T
         upper[:rank, :rank] = s_out[...]
         upper[:rank, rank:] = y_out[...]
@@ -331,8 +349,6 @@
             pltpu.VMEM((2 * rank, 2 * rank), F32),
             pltpu.VMEM((2 * rank, 2 * rank), F32),
             pltpu.VMEM((2 * rank, 2 * rank), F32),
-            pltpu.VMEM((rank // 2, 2 * rank), F32),
-            pltpu.VMEM((rank // 2, 3 * rank // 2), F32),
             pltpu.VMEM((2, rank // 4, rank // 4), F32),
             pltpu.VMEM((2, rank // 4, rank // 4), F32),
             pltpu.VMEM((2, rank // 4, rank // 2), F32),

time: 75.5 us -> 66.8 us (0.88)
  Pallas kernels: 74 us -> 65.3 us
    pallas_call x1, Pallas kernels: 74 us -> 65.3 us  [body(): pl.pallas_call(functools.partial(kernel, groups, rank), out_shape=jax.Sha...]
where the time goes in v2:
time: 66.8 us; the launch traced here: 66.6 us
  Pallas kernels  65.3 us (98%)
  local copies, waits for them, and re-layouts  1.32 us (2%)
    pallas_call x1, Pallas kernels, body(): pl.pallas_call(functools.partial(kernel, groups, rank), out_shape=jax.Sha...  65.3 us

profile of v2, /device:TPU:1, one launch (start us, length us, event | category | flops | bytes accessed | tf_op | source)
XLA Modules:
  0.0 66.6 jit_solution(9753073989723096033)
XLA Ops:
  0.0 65.3 %shard_map.46 = f32[16,256]{1,0:T(8,128)} custom-call(f32[1,256,256]{2,1,0:T(8,128)} %leaf_s.1, f32[1,256,256]{2,1,0:T(8,128)} %leaf_y.1, bf16[1,512,512]{2,1,0:T(8,128)(2,1)} %base.1, bf16[1,256,256]{2,1,0:T(8,128)(2,1)} %link.1), custom_call_target="tpu_custom_call" | custom-call | tf_op jit(solution)/shard_map/pallas_call | solution.py:338
  65.3 1.3 %copy.6 = f32[16,256]{1,0:T(8,128)} copy(f32[16,256]{1,0:T(8,128)} %shard_map.46) | data formatting | bytes 32768

commit v3 on v2

--- a/solution.py
+++ b/solution.py
@@ -176,14 +176,17 @@
     lane = lax.broadcasted_iota(jnp.int32, (small, half), 1)
     eye = jnp.where(same, 1.0, 0.0).astype(F32)
 
-    def factor():
+    def factor(partial):
         diag = upper[:half, :half]
         for part in (0, 1):
             first = eliminate(jnp.where(lane < small, diag[:small], eye), small, 0)[:, small:]
             lead[part] = first
             top = dot_full(first, diag[:small])
             joint[part] = top
-            rest = diag[small:] - dot_full_t(top[:, small:], top)
+            flipped = lax.dot_general(
+                diag[small:, :small], first, (((1,), (1,)), ((), ())), preferred_element_type=F32, precision=HIGH
+            )
+            rest = diag[small:] - dot_full(flipped, top)
             second = eliminate(jnp.where(lane < small, eye, rest), small, small)[:, :small]
             trail[part] = second
             if part == 0:
@@ -196,6 +199,9 @@
                 side = upper[:half, rank:]
             else:
                 side = upper[half:rank, rank:] - dot_full_t(reach[...], vee[:half, :])
+                if partial:
+                    mix[:half, :rank] = upper[rank : rank + half, rank:] - dot_full_t(vee[:half, :half], vee[:half, :])
+                    mix[half:rank, half:rank] = upper[rank + half :, rank + half :] - dot_full_t(vee[:half, half:], vee[:half, half:])
             across = dot_full(first, side[:small])
             low = dot_full(second, side[small:] - dot_full_t(top[:, small:], across))
             vee[part * half : part * half + small, :] = across
@@ -250,7 +256,7 @@
         hi, mid, low = pieces(mix[:, rank:], 3)
         upper[:rank, rank:] = dot(w_t[:rank, :], low) + dot(w_t[:rank, :], mid) + dot(w_t[:rank, :], hi)
         upper[rank:, rank:] = dot(w_t[rank:, :], low) + dot(w_t[rank:, :], mid) + dot(w_t[rank:, :], hi)
-        factor()
+        factor(True)
 
         @pl.when(odd)
         def _():
@@ -261,13 +267,13 @@
                         extra = extra | (me == owner + sign * (1 << bit) // 2 + 1)
             pl.semaphore_wait(barrier, jnp.where(extra, 2, 1))
 
-        s_out[:half, :] = upper[rank : rank + half, rank:] - dot_full_t(vee[:, :half], vee[...])
+        s_out[:half, :] = mix[:half, :rank] - dot_full_t(vee[half:, :half], vee[half:, :])
 
         @pl.when(me != root)
         def _():
             up_s_copies[0].start()
 
-        s_out[half:, half:] = upper[rank + half :, rank + half :] - dot_full_t(vee[:, half:], vee[:, half:])
+        s_out[half:, half:] = mix[half:rank, half:rank] - dot_full_t(vee[half:, half:], vee[half:, half:])
 
         @pl.when(me != root)
         def _():
@@ -297,7 +303,7 @@
         s_out[half:, :half] = s_out[:half, half:].T
         upper[:rank, :rank] = s_out[...]
         upper[:rank, rank:] = y_out[...]
-        factor()
+        factor(False)
         inverses((1, 0))
         low = dot_near(linv[1], vee[half:, :], 0)
         xs[half:, :] = low

time: 66.8 us -> 66.2 us (level)
  no operation moved by 1% of the time
where the time goes in v3:
time: 66.2 us; the launch traced here: 66 us
  Pallas kernels  64.7 us (98%)
  local copies, waits for them, and re-layouts  1.32 us (2%)
    pallas_call x1, Pallas kernels, body(): pl.pallas_call(functools.partial(kernel, groups, rank), out_shape=jax.Sha...  64.7 us
    unnamed x1, local copies, waits for them, and re-layouts  1.32 us

profile of v3, /device:TPU:1, one launch (start us, length us, event | category | flops | bytes accessed | tf_op | source)
XLA Modules:
  0.0 66.0 jit_solution(1432354483144306862)
XLA Ops:
  0.0 64.7 %shard_map.46 = f32[16,256]{1,0:T(8,128)} custom-call(f32[1,256,256]{2,1,0:T(8,128)} %leaf_s.1, f32[1,256,256]{2,1,0:T(8,128)} %leaf_y.1, bf16[1,512,512]{2,1,0:T(8,128)(2,1)} %base.1, bf16[1,256,256]{2,1,0:T(8,128)(2,1)} %link.1), custom_call_target="tpu_custom_call" | custom-call | tf_op jit(solution)/shard_map/pallas_call | solution.py:344
  64.7 1.3 %copy.6 = f32[16,256]{1,0:T(8,128)} copy(f32[16,256]{1,0:T(8,128)} %shard_map.46) | data formatting | bytes 32768

commit v4 on v3

--- a/solution.py
+++ b/solution.py
@@ -120,7 +120,10 @@
             device_id={"grp": group}, device_id_type=pl.DeviceIdType.MESH,
         )
 
-    cuts = ((pl.ds(0, half), pl.ds(0, rank)), (pl.ds(half, half), pl.ds(half, half)))
+    quarter = half // 2
+    cuts = (
+        (pl.ds(0, quarter), pl.ds(0, rank)), (pl.ds(quarter, quarter), pl.ds(0, rank)), (pl.ds(half, half), pl.ds(half, half))
+    )
 
     def s_copies(src, sems, slot, group):
         return [
@@ -129,7 +132,7 @@
         ]
 
     leaf_s_copies = s_copies(leaf_s.at[0], leaf_send, 0, me + 1)
-    leaf_y_copy = remote(leaf_y.at[0], y_in.at[0], leaf_send.at[2], y_recv.at[0], me + 1)
+    leaf_y_copy = remote(leaf_y.at[0], y_in.at[0], leaf_send.at[3], y_recv.at[0], me + 1)
     up_s_copies = s_copies(s_out, s_send, second, target)
     up_y_copy = remote(y_out, y_in.at[second], y_send, y_recv.at[second], target)
     own_s = pltpu.make_async_copy(leaf_s.at[0], s_in.at[1], local_sem.at[0])
@@ -234,11 +237,13 @@
             arrivals = s_copies(s_out, s_send, slot, target)
             for k in (0, 1):
                 if slot == 0:
-                    arrivals[k].wait_recv()
+                    for copy in arrivals[2 * k : 2 + k]:
+                        copy.wait_recv()
                 else:
                     @pl.when(jnp.logical_not(odd))
                     def _():
-                        arrivals[k].wait_recv()
+                        for copy in arrivals[2 * k : 2 + k]:
+                            copy.wait_recv()
 
                     if k == 0:
                         @pl.when(odd)
@@ -267,17 +272,19 @@
                         extra = extra | (me == owner + sign * (1 << bit) // 2 + 1)
             pl.semaphore_wait(barrier, jnp.where(extra, 2, 1))
 
-        s_out[:half, :] = mix[:half, :rank] - dot_full_t(vee[half:, :half], vee[half:, :])
+        for k in (0, 1):
+            now = slice(k * quarter, (k + 1) * quarter)
+            s_out[now, :] = mix[now, :rank] - dot_full_t(vee[half:, now], vee[half:, :])
+
+            @pl.when(me != root)
+            def _():
+                up_s_copies[k].start()
+
+        s_out[half:, half:] = mix[half:rank, half:rank] - dot_full_t(vee[half:, half:], vee[half:, half:])
 
         @pl.when(me != root)
         def _():
-            up_s_copies[0].start()
-
-        s_out[half:, half:] = mix[half:rank, half:rank] - dot_full_t(vee[half:, half:], vee[half:, half:])
-
-        @pl.when(me != root)
-        def _():
-            up_s_copies[1].start()
+            up_s_copies[2].start()
 
         remote(y_out, y_in.at[0], y_send, y_recv.at[0], target).wait_recv()
 
@@ -366,11 +373,11 @@
             pltpu.VMEM((rank, width), F32),
             pltpu.VMEM((rank // groups, width), F32),
             pltpu.SemaphoreType.DMA((4,)),
-            pltpu.SemaphoreType.DMA((2,)),
-            pltpu.SemaphoreType.DMA((2, 2)),
+            pltpu.SemaphoreType.DMA((3,)),
+            pltpu.SemaphoreType.DMA((2, 3)),
             pltpu.SemaphoreType.DMA,
             pltpu.SemaphoreType.DMA((2,)),
-            pltpu.SemaphoreType.DMA((3,)),
+            pltpu.SemaphoreType.DMA((4,)),
             pltpu.SemaphoreType.DMA((groups,)),
             pltpu.SemaphoreType.DMA,
         ],

time: 66.2 us -> 66.2 us (level)
  no operation moved by 1% of the time
where the time goes in v4:
time: 66.2 us; the launch traced here: 66 us
  Pallas kernels  64.7 us (98%)
  local copies, waits for them, and re-layouts  1.32 us (2%)
    pallas_call x1, Pallas kernels, body(): pl.pallas_call(functools.partial(kernel, groups, rank), out_shape=jax.Sha...  64.7 us
    unnamed x1, local copies, waits for them, and re-layouts  1.32 us

profile of v4, /device:TPU:1, one launch (start us, length us, event | category | flops | bytes accessed | tf_op | source)
XLA Modules:
  0.0 66.0 jit_solution(15398146694254652018)
XLA Ops:
  0.0 64.7 %shard_map.46 = f32[16,256]{1,0:T(8,128)} custom-call(f32[1,256,256]{2,1,0:T(8,128)} %leaf_s.1, f32[1,256,256]{2,1,0:T(8,128)} %leaf_y.1, bf16[1,512,512]{2,1,0:T(8,128)(2,1)} %base.1, bf16[1,256,256]{2,1,0:T(8,128)(2,1)} %link.1), custom_call_target="tpu_custom_call" | custom-call | tf_op jit(solution)/shard_map/pallas_call | solution.py:351
  64.7 1.3 %copy.6 = f32[16,256]{1,0:T(8,128)} copy(f32[16,256]{1,0:T(8,128)} %shard_map.46) | data formatting | bytes 32768
